TPU v7x, 32 devices: a whole 2x2x4 slice. The times are simulated.
32 devices in a mesh: seq: 4 (over y, x), head: 8 (over z, core).
Axes of the slice: x: 2, y: 2, z: 4, core: 2. Of those that a mesh axis runs over, the one named last changes fastest.
Arguments:
- queries: bfloat16 [6144, 4096], P(('seq', 'head')), may hold values from -48 to 48
- keys: bfloat16 [6144, 2048], P(('seq', 'head')), may hold values from -4 to 4
- values: bfloat16 [6144, 2048], P(('seq', 'head')), may hold values from -6 to 6
- grad_out: bfloat16 [6144, 4096], P(('seq', 'head')), may hold values from -6 to 6
- doc_lengths: int32 [16], replicated, may hold values from 1 to 1536, 6144 in all
Outputs:
- grad_queries: bfloat16 [6144, 4096], P(('seq', 'head'))
- grad_keys: bfloat16 [6144, 2048], P(('seq', 'head'))
- grad_values: bfloat16 [6144, 2048], P(('seq', 'head'))
Inputs may be any that keep to these rules, and one draw needn't show every extreme that they name: `doc_lengths`: the lengths sum to 6144.
All inputs are finite; a program needn't handle non-finite values.
Results may differ from a plain program's by a relative error of at most 0.012.
Values may be sent and summed in bfloat16 or wider, within the bound.
No kernel may reach another device: no remote copies, remote signals or barrier semaphores. Data moves between devices by JAX's collectives and lax.ppermute only.
A program may use at most 128 MiB of HBM per device.

v0:
```python
import jax
import jax.numpy as jnp
from jax import lax
from jax.sharding import PartitionSpec as P

HD = 128
WINDOW = 1024
QBLK = 512


def passed_along(shard, axis, by):
    count = lax.axis_size(axis)
    pairs = [(i, i + by) for i in range(count) if 0 <= i + by < count]
    return lax.ppermute(shard, axis, pairs)


def doc_index(doc_lengths, positions):
    doc_ends = jnp.cumsum(doc_lengths)
    return jnp.sum((positions[:, None] >= doc_ends[None, :]).astype(jnp.int32), axis=1)


def tile_grads(q_rows, out_rows, key_rows, value_rows, allowed):
    scaling = HD ** (-0.5)
    row_count = q_rows.shape[0]
    kv_count = key_rows.shape[1]
    per_group = q_rows.shape[1] // kv_count
    q_four = q_rows.reshape(row_count, kv_count, per_group, HD)
    out_four = out_rows.reshape(row_count, kv_count, per_group, HD)
    scores = (
        jnp.einsum("qagd,kad->agqk", q_four, key_rows, preferred_element_type=jnp.float32) * scaling
    )
    scores = jnp.where(allowed[None, None], scores, -jnp.inf)
    row_max = jnp.max(scores, axis=3, keepdims=True)
    exponent = jnp.exp(scores - row_max)
    weights = exponent / jnp.sum(exponent, axis=3, keepdims=True)
    weights_b = weights.astype(jnp.bfloat16)
    grad_values = jnp.einsum(
        "agqk,qagd->kad", weights_b, out_four, preferred_element_type=jnp.float32
    )
    grad_weights = jnp.einsum(
        "qagd,kad->agqk", out_four, value_rows, preferred_element_type=jnp.float32
    )
    row_dot = jnp.sum(weights * grad_weights, axis=3, keepdims=True)
    grad_scores = (weights * (grad_weights - row_dot) * scaling).astype(jnp.bfloat16)
    grad_query = jnp.einsum(
        "agqk,kad->qagd", grad_scores, key_rows, preferred_element_type=jnp.float32
    )
    grad_keys = jnp.einsum(
        "agqk,qagd->kad", grad_scores, q_four, preferred_element_type=jnp.float32
    )
    return (grad_query.reshape(row_count, kv_count * per_group, HD), grad_keys, grad_values)


def block_pass(count, q_all, out_all, key_src, value_src, src_offset, q_docs, k_docs, group_first):
    span = QBLK + WINDOW
    q_iota = jnp.arange(QBLK, dtype=jnp.int32)
    k_iota = jnp.arange(span, dtype=jnp.int32)

    def advance(totals, block):
        key_total, value_total = totals
        first_row = block * QBLK
        key_first = first_row - src_offset
        q_rows = lax.dynamic_slice_in_dim(q_all, first_row, QBLK, 0)
        out_rows = lax.dynamic_slice_in_dim(out_all, first_row, QBLK, 0)
        key_rows = lax.dynamic_slice_in_dim(key_src, key_first, span, 0)
        value_rows = lax.dynamic_slice_in_dim(value_src, key_first, span, 0)
        q_pos = group_first + first_row + q_iota
        k_pos = group_first + first_row - WINDOW + k_iota
        q_doc = lax.dynamic_slice_in_dim(q_docs, first_row, QBLK, 0)
        k_doc = lax.dynamic_slice_in_dim(k_docs, first_row, span, 0)
        allowed = (q_doc[:, None] == k_doc[None, :]) & (k_pos[None, :] <= q_pos[:, None])
        allowed = allowed & (q_pos[:, None] - k_pos[None, :] < WINDOW) & (k_pos[None, :] >= 0)
        grad_query, grad_keys, grad_values = tile_grads(
            q_rows, out_rows, key_rows, value_rows, allowed
        )
        key_total = lax.dynamic_update_slice_in_dim(
            key_total,
            lax.dynamic_slice_in_dim(key_total, key_first, span, 0) + grad_keys,
            key_first,
            0,
        )
        value_total = lax.dynamic_update_slice_in_dim(
            value_total,
            lax.dynamic_slice_in_dim(value_total, key_first, span, 0) + grad_values,
            key_first,
            0,
        )
        return ((key_total, value_total), grad_query)

    zeros_src = jnp.zeros(key_src.shape, jnp.float32)
    totals, grad_query = lax.scan(
        advance, (zeros_src, zeros_src), jnp.arange(count, dtype=jnp.int32)
    )
    return (totals[0], totals[1], grad_query.reshape((count * QBLK,) + q_all.shape[1:]))


def attend(queries, keys, values, grad_out, doc_lengths):
    group = queries.shape[0]
    group_first = lax.axis_index("seq") * group
    rims = jnp.stack([keys[group - WINDOW :], values[group - WINDOW :]])
    earlier = passed_along(rims, "seq", 1)
    key_ext = jnp.concatenate([earlier[0], keys], axis=0)
    value_ext = jnp.concatenate([earlier[1], values], axis=0)
    q_docs = doc_index(doc_lengths, group_first + jnp.arange(group, dtype=jnp.int32))
    k_docs = doc_index(
        doc_lengths, group_first - WINDOW + jnp.arange(group + WINDOW, dtype=jnp.int32)
    )
    blocks = group // QBLK
    key_total, value_total, grad_query = block_pass(
        blocks, queries, grad_out, key_ext, value_ext, 0, q_docs, k_docs, group_first
    )
    rim_keys = key_total[:WINDOW]
    rim_values = value_total[:WINDOW]
    own_keys = key_total[WINDOW:]
    own_values = value_total[WINDOW:]
    returned = passed_along(
        jnp.stack([rim_keys, rim_values]).astype(jnp.bfloat16), "seq", -1
    ).astype(jnp.float32)
    tail_keys = own_keys[group - WINDOW :] + returned[0]
    tail_values = own_values[group - WINDOW :] + returned[1]
    grad_keys = jnp.concatenate([own_keys[: group - WINDOW], tail_keys], axis=0).astype(
        jnp.bfloat16
    )
    grad_values = jnp.concatenate([own_values[: group - WINDOW], tail_values], axis=0).astype(
        jnp.bfloat16
    )
    return (grad_query.astype(jnp.bfloat16), grad_keys, grad_values)


def local(queries, keys, values, grad_out, doc_lengths):
    head_query, head_keys, head_values, head_out = (
        lax.all_to_all(queries, "head", split_axis=1, concat_axis=0, tiled=True),
        lax.all_to_all(keys, "head", split_axis=1, concat_axis=0, tiled=True),
        lax.all_to_all(values, "head", split_axis=1, concat_axis=0, tiled=True),
        lax.all_to_all(grad_out, "head", split_axis=1, concat_axis=0, tiled=True),
    )
    group = head_query.shape[0]
    grad_query, grad_keys, grad_values = attend(
        head_query.reshape(group, -1, HD),
        head_keys.reshape(group, -1, HD),
        head_values.reshape(group, -1, HD),
        head_out.reshape(group, -1, HD),
        doc_lengths,
    )
    return (
        lax.all_to_all(
            grad_query.reshape(group, -1), "head", split_axis=0, concat_axis=1, tiled=True
        ),
        lax.all_to_all(
            grad_keys.reshape(group, -1), "head", split_axis=0, concat_axis=1, tiled=True
        ),
        lax.all_to_all(
            grad_values.reshape(group, -1), "head", split_axis=0, concat_axis=1, tiled=True
        ),
    )


def solution(mesh):
    return jax.shard_map(
        local,
        mesh=mesh,
        in_specs=(
            P(("seq", "head"), None),
            P(("seq", "head"), None),
            P(("seq", "head"), None),
            P(("seq", "head"), None),
            P(),
        ),
        out_specs=(P(("seq", "head"), None), P(("seq", "head"), None), P(("seq", "head"), None)),
        check_vma=False,
    )
```

profile of v0, /device:TPU:13, one launch (start us, length us, event | category | flops | bytes accessed | tf_op | source)
XLA Modules:
  0.0 514.4 jit_solution(5997579257809941612)
XLA Ops:
  9.5 16.5 %all-to-all-done.1 = bf16[192,8,256]{2,0,1:T(8,128)(2,1)S(1)} async-done(((bf16[192,8,256]{2,0,1:T(8,128)(2,1)}), bf16[192,8,256]{2,0,1:T(8,128)(2,1)S(1)}, u32[]{:S(2)}, u32[]{:S(2)}) %all-to-all-start.1) | async-done | bytes 786464 | tf_op jit(solution)/shard_map/all_to_all | solution.py:133
  26.0 7.0 %all-to-all-start.2 = ((bf16[192,8,256]{2,0,1:T(8,128)(2,1)}), bf16[192,8,256]{2,0,1:T(8,128)(2,1)S(1)}, u32[]{:S(2)}, u32[]{:S(2)}) async-start(bf16[192,8,256]{2,0,1:T(8,128)(2,1)} %bitcast.153), calls=%async_computation.2 | async-start | bytes 1572864 | tf_op jit(solution)/shard_map/all_to_all | solution.py:134
  34.3 16.1 %all-to-all-done.2 = bf16[192,8,256]{2,0,1:T(8,128)(2,1)S(1)} async-done(((bf16[192,8,256]{2,0,1:T(8,128)(2,1)}), bf16[192,8,256]{2,0,1:T(8,128)(2,1)S(1)}, u32[]{:S(2)}, u32[]{:S(2)}) %all-to-all-start.2) | async-done | bytes 786464 | tf_op jit(solution)/shard_map/all_to_all | solution.py:134
  51.3 7.1 %all-to-all-start = ((bf16[192,8,512]{2,0,1:T(8,128)(2,1)}), bf16[192,8,512]{2,0,1:T(8,128)(2,1)S(1)}, u32[]{:S(2)}, u32[]{:S(2)}) async-start(bf16[192,8,512]{2,0,1:T(8,128)(2,1)} %bitcast.152), calls=%async_computation | async-start | bytes 3145728 | tf_op jit(solution)/shard_map/all_to_all | solution.py:132
  61.1 31.6 %all-to-all-done = bf16[192,8,512]{2,0,1:T(8,128)(2,1)S(1)} async-done(((bf16[192,8,512]{2,0,1:T(8,128)(2,1)}), bf16[192,8,512]{2,0,1:T(8,128)(2,1)S(1)}, u32[]{:S(2)}, u32[]{:S(2)}) %all-to-all-start) | async-done | bytes 1572896 | tf_op jit(solution)/shard_map/all_to_all | solution.py:132
  92.6 7.8 %all-to-all-start.3 = ((bf16[192,8,512]{2,0,1:T(8,128)(2,1)}), bf16[192,8,512]{2,0,1:T(8,128)(2,1)}, u32[]{:S(2)}, u32[]{:S(2)}) async-start(bf16[192,8,512]{2,0,1:T(8,128)(2,1)} %bitcast.151), calls=%async_computation.3 | async-start | bytes 3145728 | tf_op jit(solution)/shard_map/all_to_all | solution.py:135
  109.7 23.6 %collective-permute-done = bf16[2,1024,2,128]{3,2,1,0:T(2,128)(2,1)S(1)} collective-permute-done((bf16[2,1024,2,128]{3,2,1,0:T(2,128)(2,1)}, bf16[2,1024,2,128]{3,2,1,0:T(2,128)(2,1)S(1)}, u32[]{:S(2)}, u32[]{:S(2)}) %collective-permute-start) | collective-permute-done | bytes 1048608 | tf_op jit(solution)/shard_map/ppermute | solution.py:14
  134.0 13.1 %pad_maximum_fusion = bf16[2560,2,128]{2,1,0:T(2,128)(2,1)S(1)} fusion(bf16[1536,2,128]{2,1,0:T(2,128)(2,1)S(1)} %reshape.233, bf16[1024,2,128]{2,1,0:T(2,128)(2,1)S(1)} %get-tuple-element.277), kind=kLoop, calls=%fused_computation.51 | loop fusion | flops 655360 | bytes 2621440 | tf_op jit(solution)/shard_map/concatenate | solution.py:102
  147.0 13.1 %pad_maximum_fusion.1 = bf16[2560,2,128]{2,1,0:T(2,128)(2,1)S(1)} fusion(bf16[1536,2,128]{2,1,0:T(2,128)(2,1)S(1)} %reshape.234, bf16[1024,2,128]{2,1,0:T(2,128)(2,1)S(1)} %get-tuple-element.276), kind=kLoop, calls=%fused_computation.52 | loop fusion | flops 655360 | bytes 2621440 | tf_op jit(solution)/shard_map/concatenate | solution.py:103
  170.9 215.4 %while.17 = (s32[]{:T(128)}, f32[2560,2,128]{0,2,1:T(8,128)}, f32[2560,2,128]{0,2,1:T(8,128)}, bf16[3,512,4,128]{1,3,2,0:T(8,128)(2,1)}, s32[3]{0:T(128)S(1)}, /...) while((s32[]{:T(128)}, f32[2560,2,128]{0,2,1:T(8,128)}, ...), condition=%wide.region_7.8_spmd.clone, body=%wide.region_3.7_spmd.clone.sunk | while | flops 4095751680 | bytes 147148672 | solution.py:91
  179.2 10.5 %fusion.70 = (f32[2,2,512]{2,1,0:T(2,128)S(1)}, f32[2,2,512,1536]{2,3,1,0:T(8,128)}) fusion(pred[512,1536]{0,1:T(8,128)(4,1)} %fusion.69, bf16[512,2,2,128]{3,0,2,1:T(8,128)(2,1)} %bitcast.193, bf16[1536,2,128]{2,1,0:T(2,128)(2,1)} %get-tuple-element.362), kind=kOutput, calls=%fused_computation.75.clone.1 | convolution fusion | flops 817890816 | bytes 14688256 | tf_op jit(solution)/shard_map/while/body/eval_jaxpr/sub | solution.py:34
  189.8 6.3 %fusion.68 = f32[2,1536,512,2]{2,1,3,0:T(8,128)} fusion(bf16[512,2,2,128]{3,0,2,1:T(8,128)(2,1)S(1)} %bitcast.191, bf16[1536,2,128]{2,1,0:T(2,128)(2,1)S(1)} %get-tuple-element.361), kind=kOutput, calls=%fused_computation.32.clone.1 | convolution fusion | flops 805306368 | bytes 13893632 | tf_op jit(solution)/shard_map/while/body/eval_jaxpr/qagd,kad->agqk/dot_general | solution.py:40
  196.1 17.8 %fusion.73 = bf16[2,128,2,512]{3,1,2,0:T(8,128)(2,1)S(1)} fusion(f32[2,1536,512,2]{2,1,3,0:T(8,128)} %fusion.68, bf16[1536,2,128]{2,1,0:T(2,128)(2,1)} %get-tuple-element.362, f32[2,2,512,1536]{2,3,1,0:T(8,128)} %get-tuple-element.363, f32[2,2,512]{2,1,0:T(2,128)S(1)} %get-tuple-element.364), kind=kOutput, calls=%fused_computation.19.clone.1 | convolution fusion | flops 827330048 | bytes 26484736 | tf_op jit(solution)/shard_map/while/body/eval_jaxpr/agqk,kad->qagd/dot_general | solution.py:45
  214.8 8.5 %fusion.72 = f32[2560,2,128]{0,2,1:T(8,128)} fusion(f32[2560,2,128]{0,2,1:T(8,128)} %get-tuple-element.385, s32[]{:T(128)S(6)} %select_n.44, bf16[512,2,2,128]{3,0,2,1:T(8,128)(2,1)S(1)} %bitcast.192, f32[2,2,512,1536]{2,3,1,0:T(8,128)} %get-tuple-element.363, f32[2,2,512]{2,1,0:T(2,128)S(1)} %get-tuple-element.364), kind=kOutput, calls=%fused_computation.26.clone.1 | convolution fusion | flops 811991040 | bytes 16261124 | tf_op jit(solution)/shard_map/while/body/eval_jaxpr/agqk,qagd->kad/dot_general | solution.py:37
  223.3 19.5 %fusion.71 = f32[2560,2,128]{0,2,1:T(8,128)} fusion(f32[2560,2,128]{0,2,1:T(8,128)} %get-tuple-element.384, s32[]{:T(128)S(6)} %select_n.44, bf16[512,2,2,128]{3,0,2,1:T(8,128)(2,1)S(1)} %bitcast.194, f32[2,1536,512,2]{2,1,3,0:T(8,128)} %fusion.68, f32[2,2,512,1536]{2,3,1,0:T(8,128)} %get-tuple-element.363, f32[2,2,512]{2,1,0:T(2,128)S(1)} %get-tuple-element.364), kind=kOutput, calls=%fused_computation.29.clone.1 | convolution fusion | flops 827723264 | bytes 54018052 | tf_op jit(solution)/shard_map/while/body/eval_jaxpr/agqk,qagd->kad/dot_general | solution.py:48
  251.1 10.5 %fusion.70 = (f32[2,2,512]{2,1,0:T(2,128)S(1)}, f32[2,2,512,1536]{2,3,1,0:T(8,128)}) fusion(pred[512,1536]{0,1:T(8,128)(4,1)} %fusion.69, bf16[512,2,2,128]{3,0,2,1:T(8,128)(2,1)} %bitcast.193, bf16[1536,2,128]{2,1,0:T(2,128)(2,1)} %get-tuple-element.362), kind=kOutput, calls=%fused_computation.75.clone.1 | convolution fusion | flops 817890816 | bytes 14688256 | tf_op jit(solution)/shard_map/while/body/eval_jaxpr/sub | solution.py:34
  261.6 6.3 %fusion.68 = f32[2,1536,512,2]{2,1,3,0:T(8,128)} fusion(bf16[512,2,2,128]{3,0,2,1:T(8,128)(2,1)S(1)} %bitcast.191, bf16[1536,2,128]{2,1,0:T(2,128)(2,1)S(1)} %get-tuple-element.361), kind=kOutput, calls=%fused_computation.32.clone.1 | convolution fusion | flops 805306368 | bytes 13893632 | tf_op jit(solution)/shard_map/while/body/eval_jaxpr/qagd,kad->agqk/dot_general | solution.py:40
  268.0 17.8 %fusion.73 = bf16[2,128,2,512]{3,1,2,0:T(8,128)(2,1)S(1)} fusion(f32[2,1536,512,2]{2,1,3,0:T(8,128)} %fusion.68, bf16[1536,2,128]{2,1,0:T(2,128)(2,1)} %get-tuple-element.362, f32[2,2,512,1536]{2,3,1,0:T(8,128)} %get-tuple-element.363, f32[2,2,512]{2,1,0:T(2,128)S(1)} %get-tuple-element.364), kind=kOutput, calls=%fused_computation.19.clone.1 | convolution fusion | flops 827330048 | bytes 26484736 | tf_op jit(solution)/shard_map/while/body/eval_jaxpr/agqk,kad->qagd/dot_general | solution.py:45
  286.6 8.5 %fusion.72 = f32[2560,2,128]{0,2,1:T(8,128)} fusion(f32[2560,2,128]{0,2,1:T(8,128)} %get-tuple-element.385, s32[]{:T(128)S(6)} %select_n.44, bf16[512,2,2,128]{3,0,2,1:T(8,128)(2,1)S(1)} %bitcast.192, f32[2,2,512,1536]{2,3,1,0:T(8,128)} %get-tuple-element.363, f32[2,2,512]{2,1,0:T(2,128)S(1)} %get-tuple-element.364), kind=kOutput, calls=%fused_computation.26.clone.1 | convolution fusion | flops 811991040 | bytes 16261124 | tf_op jit(solution)/shard_map/while/body/eval_jaxpr/agqk,qagd->kad/dot_general | solution.py:37
  295.1 19.4 %fusion.71 = f32[2560,2,128]{0,2,1:T(8,128)} fusion(f32[2560,2,128]{0,2,1:T(8,128)} %get-tuple-element.384, s32[]{:T(128)S(6)} %select_n.44, bf16[512,2,2,128]{3,0,2,1:T(8,128)(2,1)S(1)} %bitcast.194, f32[2,1536,512,2]{2,1,3,0:T(8,128)} %fusion.68, f32[2,2,512,1536]{2,3,1,0:T(8,128)} %get-tuple-element.363, f32[2,2,512]{2,1,0:T(2,128)S(1)} %get-tuple-element.364), kind=kOutput, calls=%fused_computation.29.clone.1 | convolution fusion | flops 827723264 | bytes 54018052 | tf_op jit(solution)/shard_map/while/body/eval_jaxpr/agqk,qagd->kad/dot_general | solution.py:48
  322.8 10.5 %fusion.70 = (f32[2,2,512]{2,1,0:T(2,128)S(1)}, f32[2,2,512,1536]{2,3,1,0:T(8,128)}) fusion(pred[512,1536]{0,1:T(8,128)(4,1)} %fusion.69, bf16[512,2,2,128]{3,0,2,1:T(8,128)(2,1)} %bitcast.193, bf16[1536,2,128]{2,1,0:T(2,128)(2,1)} %get-tuple-element.362), kind=kOutput, calls=%fused_computation.75.clone.1 | convolution fusion | flops 817890816 | bytes 14688256 | tf_op jit(solution)/shard_map/while/body/eval_jaxpr/sub | solution.py:34
  333.4 6.3 %fusion.68 = f32[2,1536,512,2]{2,1,3,0:T(8,128)} fusion(bf16[512,2,2,128]{3,0,2,1:T(8,128)(2,1)S(1)} %bitcast.191, bf16[1536,2,128]{2,1,0:T(2,128)(2,1)S(1)} %get-tuple-element.361), kind=kOutput, calls=%fused_computation.32.clone.1 | convolution fusion | flops 805306368 | bytes 13893632 | tf_op jit(solution)/shard_map/while/body/eval_jaxpr/qagd,kad->agqk/dot_general | solution.py:40
  339.7 17.8 %fusion.73 = bf16[2,128,2,512]{3,1,2,0:T(8,128)(2,1)S(1)} fusion(f32[2,1536,512,2]{2,1,3,0:T(8,128)} %fusion.68, bf16[1536,2,128]{2,1,0:T(2,128)(2,1)} %get-tuple-element.362, f32[2,2,512,1536]{2,3,1,0:T(8,128)} %get-tuple-element.363, f32[2,2,512]{2,1,0:T(2,128)S(1)} %get-tuple-element.364), kind=kOutput, calls=%fused_computation.19.clone.1 | convolution fusion | flops 827330048 | bytes 26484736 | tf_op jit(solution)/shard_map/while/body/eval_jaxpr/agqk,kad->qagd/dot_general | solution.py:45
  358.3 8.6 %fusion.72 = f32[2560,2,128]{0,2,1:T(8,128)} fusion(f32[2560,2,128]{0,2,1:T(8,128)} %get-tuple-element.385, s32[]{:T(128)S(6)} %select_n.44, bf16[512,2,2,128]{3,0,2,1:T(8,128)(2,1)S(1)} %bitcast.192, f32[2,2,512,1536]{2,3,1,0:T(8,128)} %get-tuple-element.363, f32[2,2,512]{2,1,0:T(2,128)S(1)} %get-tuple-element.364), kind=kOutput, calls=%fused_computation.26.clone.1 | convolution fusion | flops 811991040 | bytes 16261124 | tf_op jit(solution)/shard_map/while/body/eval_jaxpr/agqk,qagd->kad/dot_general | solution.py:37
  366.9 19.4 %fusion.71 = f32[2560,2,128]{0,2,1:T(8,128)} fusion(f32[2560,2,128]{0,2,1:T(8,128)} %get-tuple-element.384, s32[]{:T(128)S(6)} %select_n.44, bf16[512,2,2,128]{3,0,2,1:T(8,128)(2,1)S(1)} %bitcast.194, f32[2,1536,512,2]{2,1,3,0:T(8,128)} %fusion.68, f32[2,2,512,1536]{2,3,1,0:T(8,128)} %get-tuple-element.363, f32[2,2,512]{2,1,0:T(2,128)S(1)} %get-tuple-element.364), kind=kOutput, calls=%fused_computation.29.clone.1 | convolution fusion | flops 827723264 | bytes 54018052 | tf_op jit(solution)/shard_map/while/body/eval_jaxpr/agqk,qagd->kad/dot_general | solution.py:48
  393.5 23.3 %collective-permute-done.1 = bf16[2,1024,2,128]{1,3,2,0:T(8,128)(2,1)} collective-permute-done((bf16[2,1024,2,128]{1,3,2,0:T(8,128)(2,1)}, bf16[2,1024,2,128]{1,3,2,0:T(8,128)(2,1)}, u32[]{:S(2)}, u32[]{:S(2)}) %collective-permute-start.1) | collective-permute-done | bytes 1048608 | tf_op jit(solution)/shard_map/ppermute | solution.py:14
  422.9 7.0 %all-to-all-start.6 = ((bf16[8,192,256]{2,1,0:T(8,128)(2,1)}), bf16[8,192,256]{2,1,0:T(8,128)(2,1)S(1)}, u32[]{:S(2)}, u32[]{:S(2)}) async-start(bf16[8,192,256]{2,1,0:T(8,128)(2,1)} %bitcast.20), calls=%async_computation.6 | async-start | bytes 1572864 | tf_op jit(solution)/shard_map/all_to_all | solution.py:152
  431.1 16.1 %all-to-all-done.6 = bf16[8,192,256]{2,1,0:T(8,128)(2,1)S(1)} async-done(((bf16[8,192,256]{2,1,0:T(8,128)(2,1)}), bf16[8,192,256]{2,1,0:T(8,128)(2,1)S(1)}, u32[]{:S(2)}, u32[]{:S(2)}) %all-to-all-start.6) | async-done | bytes 786464 | tf_op jit(solution)/shard_map/all_to_all | solution.py:152
  447.3 7.0 %all-to-all-start.5 = ((bf16[8,192,256]{2,1,0:T(8,128)(2,1)}), bf16[8,192,256]{2,1,0:T(8,128)(2,1)S(1)}, u32[]{:S(2)}, u32[]{:S(2)}) async-start(bf16[8,192,256]{2,1,0:T(8,128)(2,1)} %bitcast.15), calls=%async_computation.5 | async-start | bytes 1572864 | tf_op jit(solution)/shard_map/all_to_all | solution.py:149
  459.0 12.7 %all-to-all-done.5 = bf16[8,192,256]{2,1,0:T(8,128)(2,1)S(1)} async-done(((bf16[8,192,256]{2,1,0:T(8,128)(2,1)}), bf16[8,192,256]{2,1,0:T(8,128)(2,1)S(1)}, u32[]{:S(2)}, u32[]{:S(2)}) %all-to-all-start.5) | async-done | bytes 786464 | tf_op jit(solution)/shard_map/all_to_all | solution.py:149
  471.7 7.1 %all-to-all-start.4 = ((bf16[8,192,512]{2,1,0:T(8,128)(2,1)}), bf16[8,192,512]{2,1,0:T(8,128)(2,1)S(1)}, u32[]{:S(2)}, u32[]{:S(2)}) async-start(bf16[8,192,512]{2,1,0:T(8,128)(2,1)} %convert_element_type.45), calls=%async_computation.4 | async-start | bytes 3145728 | tf_op jit(solution)/shard_map/all_to_all | solution.py:146
  480.7 32.3 %all-to-all-done.4 = bf16[8,192,512]{2,1,0:T(8,128)(2,1)S(1)} async-done(((bf16[8,192,512]{2,1,0:T(8,128)(2,1)}), bf16[8,192,512]{2,1,0:T(8,128)(2,1)S(1)}, u32[]{:S(2)}, u32[]{:S(2)}) %all-to-all-start.4) | async-done | bytes 1572896 | tf_op jit(solution)/shard_map/all_to_all | solution.py:146
  (115 shorter events, 82.5 us)
Async XLA Ops:
  0.6 7.9 %copy-start.8 = (bf16[192,2048]{1,0:T(8,128)(2,1)S(1)}, bf16[192,2048]{1,0:T(8,128)(2,1)}, u32[]{:S(2)}) copy-start(bf16[192,2048]{1,0:T(8,128)(2,1)} %param.9) | copy-start | bytes 2359300
  2.8 30.2 %copy-start.7 = (bf16[192,4096]{1,0:T(8,128)(2,1)S(1)}, bf16[192,4096]{1,0:T(8,128)(2,1)}, u32[]{:S(2)}) copy-start(bf16[192,4096]{1,0:T(8,128)(2,1)} %param.7) | copy-start | bytes 4718596
  2.8 23.2 %all-to-all-start.1 = ((bf16[192,8,256]{2,0,1:T(8,128)(2,1)}), bf16[192,8,256]{2,0,1:T(8,128)(2,1)S(1)}, u32[]{:S(2)}, u32[]{:S(2)}) async-start(bf16[192,8,256]{2,0,1:T(8,128)(2,1)} %bitcast.154), calls=%async_computation.1 | async-start | bytes 1572864 | tf_op jit(solution)/shard_map/all_to_all | solution.py:133
  26.0 24.4 %all-to-all-start.2 = ((bf16[192,8,256]{2,0,1:T(8,128)(2,1)}), bf16[192,8,256]{2,0,1:T(8,128)(2,1)S(1)}, u32[]{:S(2)}, u32[]{:S(2)}) async-start(bf16[192,8,256]{2,0,1:T(8,128)(2,1)} %bitcast.153), calls=%async_computation.2 | async-start | bytes 1572864 | tf_op jit(solution)/shard_map/all_to_all | solution.py:134
  50.4 0.9 copy-start.6
  51.3 41.3 %all-to-all-start = ((bf16[192,8,512]{2,0,1:T(8,128)(2,1)}), bf16[192,8,512]{2,0,1:T(8,128)(2,1)S(1)}, u32[]{:S(2)}, u32[]{:S(2)}) async-start(bf16[192,8,512]{2,0,1:T(8,128)(2,1)} %bitcast.152), calls=%async_computation | async-start | bytes 3145728 | tf_op jit(solution)/shard_map/all_to_all | solution.py:132
  92.6 10.0 %copy-start.4 = (bf16[192,8,512]{2,0,1:T(8,128)(2,1)}, bf16[192,8,512]{2,0,1:T(8,128)(2,1)S(1)}, u32[]{:S(2)}) copy-start(bf16[192,8,512]{2,0,1:T(8,128)(2,1)S(1)} %all-to-all-done) | copy-start | bytes 4718596
  92.6 71.0 %all-to-all-start.3 = ((bf16[192,8,512]{2,0,1:T(8,128)(2,1)}), bf16[192,8,512]{2,0,1:T(8,128)(2,1)}, u32[]{:S(2)}, u32[]{:S(2)}) async-start(bf16[192,8,512]{2,0,1:T(8,128)(2,1)} %bitcast.151), calls=%async_computation.3 | async-start | bytes 3145728 | tf_op jit(solution)/shard_map/all_to_all | solution.py:135
  100.6 8.6 %copy-start.9 = (s32[16]{0:T(128)S(1)}, s32[16]{0:T(128)}, u32[]{:S(2)}) copy-start(s32[16]{0:T(128)} %param.11) | copy-start | bytes 196
  105.9 27.4 %collective-permute-start = (bf16[2,1024,2,128]{3,2,1,0:T(2,128)(2,1)}, bf16[2,1024,2,128]{3,2,1,0:T(2,128)(2,1)S(1)}, u32[]{:S(2)}, u32[]{:S(2)}) collective-permute-start(bf16[2,1024,2,128]{3,2,1,0:T(2,128)(2,1)} %pad_maximum_fusion.2), channel_id=1, source_target_pairs={{0,8},{8,16},{16,24},{1,9},{9,17},{17,25},{2,10},{10,18},{18,26},{... | collective-permute-start | bytes 3145736 | tf_op jit(solution)/shard_map/ppermute | solution.py:14
  170.9 5.8 %copy-start = (bf16[2560,2,128]{2,1,0:T(2,128)(2,1)}, bf16[2560,2,128]{2,1,0:T(2,128)(2,1)S(1)}, u32[]{:S(2)}) copy-start(bf16[2560,2,128]{2,1,0:T(2,128)(2,1)S(1)} %get-tuple-element.411) | copy-start | bytes 3932164 | tf_op jit(solution)/shard_map/while
  214.8 8.5 %copy-start.3 = (bf16[512,4,128]{2,0,1:T(8,128)(2,1)S(1)}, bf16[512,4,128]{2,0,1:T(8,128)(2,1)}, u32[]{:S(2)}) copy-start(bf16[512,4,128]{2,0,1:T(8,128)(2,1)} %copy.138) | copy-start | bytes 1572868 | tf_op jit(solution)/shard_map/while
  223.3 19.5 %copy-start.1 = (bf16[2560,2,128]{2,1,0:T(2,128)(2,1)S(1)}, bf16[2560,2,128]{2,1,0:T(2,128)(2,1)}, u32[]{:S(2)}) copy-start(bf16[2560,2,128]{2,1,0:T(2,128)(2,1)} %copy-done) | copy-start | bytes 3932164 | tf_op jit(solution)/shard_map/while
  242.8 5.8 %copy-start = (bf16[2560,2,128]{2,1,0:T(2,128)(2,1)}, bf16[2560,2,128]{2,1,0:T(2,128)(2,1)S(1)}, u32[]{:S(2)}) copy-start(bf16[2560,2,128]{2,1,0:T(2,128)(2,1)S(1)} %get-tuple-element.411) | copy-start | bytes 3932164 | tf_op jit(solution)/shard_map/while
  286.6 8.5 %copy-start.3 = (bf16[512,4,128]{2,0,1:T(8,128)(2,1)S(1)}, bf16[512,4,128]{2,0,1:T(8,128)(2,1)}, u32[]{:S(2)}) copy-start(bf16[512,4,128]{2,0,1:T(8,128)(2,1)} %copy.138) | copy-start | bytes 1572868 | tf_op jit(solution)/shard_map/while
  295.1 19.4 %copy-start.1 = (bf16[2560,2,128]{2,1,0:T(2,128)(2,1)S(1)}, bf16[2560,2,128]{2,1,0:T(2,128)(2,1)}, u32[]{:S(2)}) copy-start(bf16[2560,2,128]{2,1,0:T(2,128)(2,1)} %copy-done) | copy-start | bytes 3932164 | tf_op jit(solution)/shard_map/while
  314.5 5.8 %copy-start = (bf16[2560,2,128]{2,1,0:T(2,128)(2,1)}, bf16[2560,2,128]{2,1,0:T(2,128)(2,1)S(1)}, u32[]{:S(2)}) copy-start(bf16[2560,2,128]{2,1,0:T(2,128)(2,1)S(1)} %get-tuple-element.411) | copy-start | bytes 3932164 | tf_op jit(solution)/shard_map/while
  358.3 8.6 %copy-start.3 = (bf16[512,4,128]{2,0,1:T(8,128)(2,1)S(1)}, bf16[512,4,128]{2,0,1:T(8,128)(2,1)}, u32[]{:S(2)}) copy-start(bf16[512,4,128]{2,0,1:T(8,128)(2,1)} %copy.138) | copy-start | bytes 1572868 | tf_op jit(solution)/shard_map/while
  366.9 19.4 %copy-start.1 = (bf16[2560,2,128]{2,1,0:T(2,128)(2,1)S(1)}, bf16[2560,2,128]{2,1,0:T(2,128)(2,1)}, u32[]{:S(2)}) copy-start(bf16[2560,2,128]{2,1,0:T(2,128)(2,1)} %copy-done) | copy-start | bytes 3932164 | tf_op jit(solution)/shard_map/while
  386.3 2.5 copy-start.2
  389.0 1.1 copy-start.5
  391.2 25.7 %collective-permute-start.1 = (bf16[2,1024,2,128]{1,3,2,0:T(8,128)(2,1)}, bf16[2,1024,2,128]{1,3,2,0:T(8,128)(2,1)}, u32[]{:S(2)}, u32[]{:S(2)}) collective-permute-start(bf16[2,1024,2,128]{1,3,2,0:T(8,128)(2,1)} %pad_maximum_fusion.3), channel_id=1, source_target_pairs={{8,0},{16,8},{24,16},{9,1},{17,9},{25,17},{10,2},{18,10},{26,18},{... | collective-permute-start | bytes 3145736 | tf_op jit(solution)/shard_map/ppermute | solution.py:14
  420.7 9.2 %slice-start = ((bf16[2560,2,128]{0,2,1:T(8,128)(2,1)}), bf16[512,2,128]{0,2,1:T(8,128)(2,1)S(1)}, s32[]{:S(2)}) async-start(bf16[2560,2,128]{0,2,1:T(8,128)(2,1)} %copy-done.5), calls=%async_computation.7 | async-start | bytes 524288 | tf_op jit(solution)/shard_map/slice | solution.py:121
  422.9 24.4 %all-to-all-start.6 = ((bf16[8,192,256]{2,1,0:T(8,128)(2,1)}), bf16[8,192,256]{2,1,0:T(8,128)(2,1)S(1)}, u32[]{:S(2)}, u32[]{:S(2)}) async-start(bf16[8,192,256]{2,1,0:T(8,128)(2,1)} %bitcast.20), calls=%async_computation.6 | async-start | bytes 1572864 | tf_op jit(solution)/shard_map/all_to_all | solution.py:152
  447.3 24.4 %all-to-all-start.5 = ((bf16[8,192,256]{2,1,0:T(8,128)(2,1)}), bf16[8,192,256]{2,1,0:T(8,128)(2,1)S(1)}, u32[]{:S(2)}, u32[]{:S(2)}) async-start(bf16[8,192,256]{2,1,0:T(8,128)(2,1)} %bitcast.15), calls=%async_computation.5 | async-start | bytes 1572864 | tf_op jit(solution)/shard_map/all_to_all | solution.py:149
  471.7 41.3 %all-to-all-start.4 = ((bf16[8,192,512]{2,1,0:T(8,128)(2,1)}), bf16[8,192,512]{2,1,0:T(8,128)(2,1)S(1)}, u32[]{:S(2)}, u32[]{:S(2)}) async-start(bf16[8,192,512]{2,1,0:T(8,128)(2,1)} %convert_element_type.45), calls=%async_computation.4 | async-start | bytes 3145728 | tf_op jit(solution)/shard_map/all_to_all | solution.py:146
where the time goes:
time: 519 us; the launch traced here: 514 us
  matrix products  188 us (36%)
  waiting for transfers between devices  172 us (33%)
  starting transfers between devices  54.1 us (10%)
  local copies, waits for them, and re-layouts  52 us (10%)
  other arithmetic  45.4 us (9%)
    dot_general x3, matrix products, tile_grads(): jnp.einsum('agqk,qagd->kad', grad_scores, q_four, preferred_element_type=...  58.3 us
    dot_general x3, matrix products, tile_grads(): jnp.einsum('agqk,kad->qagd', grad_scores, key_rows, preferred_element_typ...  53.4 us
    ppermute x2, waiting for transfers between devices, passed_along(): return lax.ppermute(shard, axis, pairs)  46.9 us
    all_to_all x1, waiting for transfers between devices, local(): lax.all_to_all(grad_query.reshape(group, -1), 'head', split_axis=0, conca...  32.3 us
    all_to_all x1, waiting for transfers between devices, local(): lax.all_to_all(queries, 'head', split_axis=1, concat_axis=0, tiled=True)  31.6 us
    sub x3, matrix products, tile_grads(): exponent = jnp.exp(scores - row_max)  31.4 us
    dot_general x3, matrix products, tile_grads(): jnp.einsum('agqk,qagd->kad', weights_b, out_four, preferred_element_type=...  25.5 us
    dot_general x3, matrix products, tile_grads(): jnp.einsum('qagd,kad->agqk', out_four, value_rows, preferred_element_type...  19 us
  transfers between devices with their start and end apart: 9, of which 8 were waited for; matrix products, arithmetic and copies ran while one was open for 10% of the time, Pallas kernels for 0%

commit v1 on v0

v1 whole, which is shorter than its diff:
```python
import functools
import math

import jax
import jax.numpy as jnp
from jax import lax
from jax.experimental import pallas as pl
from jax.experimental.pallas import tpu as pltpu
from jax.sharding import PartitionSpec as P

HD = 128
WINDOW = 1024
TQ = 256
TK = 256
SCALING = HD ** (-0.5)
EXP2_SCALE = SCALING * math.log2(math.e)
MASKED = -1e30


def passed_along(shard, axis, by):
    count = lax.axis_size(axis)
    pairs = [(i, i + by) for i in range(count) if 0 <= i + by < count]
    return lax.ppermute(shard, axis, pairs)


def dot_nt(a, b):
    return lax.dot_general(a, b, (((1,), (1,)), ((), ())), preferred_element_type=jnp.float32)


def dot_nn(a, b):
    return lax.dot_general(a, b, (((1,), (0,)), ((), ())), preferred_element_type=jnp.float32)


def attend_kernel(
    per_group, first_tile, low_ref, qd_ref, halo_k, halo_v, own_k, own_v,
    dq_ref, own_ref, rim_ref,
    k_ext, v_ext, k_t, dk_ext, dv_ext, s_buf, dp_buf,
):
    group = qd_ref.shape[0]
    reach = WINDOW // TK
    k_ext[:WINDOW, :] = halo_k[...]
    k_ext[WINDOW:, :] = own_k[...]
    v_ext[:WINDOW, :] = halo_v[...]
    v_ext[WINDOW:, :] = own_v[...]
    dk_ext[...] = jnp.zeros_like(dk_ext)
    dv_ext[...] = jnp.zeros_like(dv_ext)

    def turn(t, carry):
        rows = pl.ds(pl.multiple_of(t * TK, TK), TK)
        k_t[t] = jnp.transpose(k_ext[rows, :].astype(jnp.float32)).astype(jnp.bfloat16)
        return carry

    lax.fori_loop(0, (group + WINDOW) // TK, turn, 0)
    wide = per_group * TQ
    key_iota = lax.broadcasted_iota(jnp.int32, (TK, wide), 0)

    def q_block(b, carry):
        q_rows = pl.ds(pl.multiple_of(b * TQ, TQ), TQ)
        start = first_tile[b]
        stop = b * (TQ // TK) + (TQ // TK - 1) + reach + 1
        q = jnp.concatenate(
            [qd_ref[q_rows, i * HD : (i + 1) * HD] for i in range(per_group)], axis=0
        )
        d_out = jnp.concatenate(
            [qd_ref[q_rows, i * HD : (i + 1) * HD] for i in range(per_group, 2 * per_group)],
            axis=0,
        )
        low = low_ref[:, q_rows]
        low = jnp.concatenate([low] * per_group, axis=1)
        high = b * TQ + WINDOW + lax.broadcasted_iota(jnp.int32, (1, TQ), 1)
        high = jnp.concatenate([high] * per_group, axis=1)

        def score(t, top):
            rows = pl.ds(pl.multiple_of(t * TK, TK), TK)
            slot = pl.ds(pl.multiple_of((t - start) * TK, TK), TK)
            s = dot_nt(k_ext[rows, :], q)
            j = key_iota + t * TK
            s = jnp.where((j >= low) & (j <= high), s, MASKED)
            s_buf[slot, :] = s
            return jnp.maximum(top, jnp.max(s, axis=0, keepdims=True))

        top = lax.fori_loop(start, stop, score, jnp.full((1, wide), MASKED, jnp.float32))

        def weigh(t, sums):
            total, dotted = sums
            rows = pl.ds(pl.multiple_of(t * TK, TK), TK)
            slot = pl.ds(pl.multiple_of((t - start) * TK, TK), TK)
            p = jnp.exp2((s_buf[slot, :] - top) * EXP2_SCALE)
            dp = dot_nt(v_ext[rows, :], d_out)
            s_buf[slot, :] = p
            dp_buf[slot, :] = dp
            return (
                total + jnp.sum(p, axis=0, keepdims=True),
                dotted + jnp.sum(p * dp, axis=0, keepdims=True),
            )

        zero = jnp.zeros((1, wide), jnp.float32)
        total, dotted = lax.fori_loop(start, stop, weigh, (zero, zero))
        inverse = 1.0 / total
        row_dot = dotted * inverse
        inverse_scaled = inverse * SCALING

        def grads(t, dq_t):
            rows = pl.ds(pl.multiple_of(t * TK, TK), TK)
            slot = pl.ds(pl.multiple_of((t - start) * TK, TK), TK)
            p = s_buf[slot, :]
            ds = ((p * inverse_scaled) * (dp_buf[slot, :] - row_dot)).astype(jnp.bfloat16)
            weights = (p * inverse).astype(jnp.bfloat16)
            dv_ext[rows, :] += dot_nn(weights, d_out)
            dk_ext[rows, :] += dot_nn(ds, q)
            return dq_t + dot_nn(k_t[t], ds)

        dq_t = lax.fori_loop(start, stop, grads, jnp.zeros((HD, wide), jnp.float32))
        dq = jnp.transpose(dq_t).astype(jnp.bfloat16)
        for i in range(per_group):
            dq_ref[q_rows, i * HD : (i + 1) * HD] = dq[i * TQ : (i + 1) * TQ, :]
        return carry

    lax.fori_loop(0, group // TQ, q_block, 0)
    rim_ref[:, :HD] = dk_ext[:WINDOW, :].astype(jnp.bfloat16)
    rim_ref[:, HD:] = dv_ext[:WINDOW, :].astype(jnp.bfloat16)
    own_ref[:, :HD] = dk_ext[WINDOW:, :]
    own_ref[:, HD:] = dv_ext[WINDOW:, :]


def attend(qd, halo, own, chunk, kv_local, low, first_tile):
    group = qd.shape[0]
    per_group = qd.shape[1] // (2 * HD)
    ext = group + WINDOW
    wide = per_group * TQ
    span = WINDOW + TQ

    def vmem(shape, lane_block=0):
        return pl.BlockSpec(shape, lambda i: (0, lane_block))

    area = group * (WINDOW + TQ) * per_group
    return pl.pallas_call(
        functools.partial(attend_kernel, per_group),
        grid=(1,),
        out_shape=(
            jax.ShapeDtypeStruct((group, per_group * HD), jnp.bfloat16),
            jax.ShapeDtypeStruct((group, 2 * HD), jnp.float32),
            jax.ShapeDtypeStruct((WINDOW, 2 * HD), jnp.bfloat16),
        ),
        in_specs=[
            pl.BlockSpec(memory_space=pltpu.SMEM),
            vmem((1, group)),
            vmem((group, 2 * per_group * HD)),
            vmem((WINDOW, HD), chunk),
            vmem((WINDOW, HD), kv_local + chunk),
            vmem((group, HD), chunk),
            vmem((group, HD), kv_local + chunk),
        ],
        out_specs=(
            vmem((group, per_group * HD)),
            vmem((group, 2 * HD)),
            vmem((WINDOW, 2 * HD)),
        ),
        scratch_shapes=[
            pltpu.VMEM((ext, HD), jnp.bfloat16),
            pltpu.VMEM((ext, HD), jnp.bfloat16),
            pltpu.VMEM((ext // TK, HD, TK), jnp.bfloat16),
            pltpu.VMEM((ext, HD), jnp.float32),
            pltpu.VMEM((ext, HD), jnp.float32),
            pltpu.VMEM((span, wide), jnp.float32),
            pltpu.VMEM((span, wide), jnp.float32),
        ],
        compiler_params=pltpu.CompilerParams(vmem_limit_bytes=40 * 1024 * 1024),
        cost_estimate=pl.CostEstimate(
            flops=area * HD * 2 * 5, bytes_accessed=group * HD * 24, transcendentals=area
        ),
        name="attend",
    )(first_tile, low, qd, halo, halo, own, own)


def to_heads(parts):
    rows = parts[0].shape[0]
    sent = jnp.concatenate([jnp.transpose(p, (1, 0, 2)) for p in parts], axis=2)
    came = lax.all_to_all(sent, "head", split_axis=0, concat_axis=0, tiled=True)
    return came.reshape(-1, sent.shape[2])


def to_tokens(rows, ways):
    sent = rows.reshape(ways, rows.shape[0] // ways, rows.shape[1])
    return lax.all_to_all(sent, "head", split_axis=0, concat_axis=0, tiled=True)


def local(queries, keys, values, grad_out, doc_lengths):
    ways = lax.axis_size("head")
    tokens = queries.shape[0]
    group = tokens * ways
    kv_local = keys.shape[1] // (ways * HD)
    per_group = queries.shape[1] // keys.shape[1]
    group_first = lax.axis_index("seq") * group

    kv = to_heads([keys.reshape(tokens, ways, -1), values.reshape(tokens, ways, -1)])
    halo = passed_along(kv[group - WINDOW :], "seq", 1)
    q_cut = queries.reshape(tokens, ways, kv_local, per_group * HD)
    o_cut = grad_out.reshape(tokens, ways, kv_local, per_group * HD)
    qds = [to_heads([q_cut[:, :, c], o_cut[:, :, c]]) for c in range(kv_local)]

    position = group_first + jnp.arange(group, dtype=jnp.int32)
    ends = jnp.cumsum(doc_lengths)
    doc_start = jnp.sum(
        jnp.where(position[:, None] >= ends[None, :], doc_lengths[None, :], 0), axis=1
    )
    low = jnp.maximum(doc_start, position - (WINDOW - 1)) - (group_first - WINDOW)
    low = low.astype(jnp.int32)
    first_tile = low[::TQ] // TK

    grads = []
    for c in range(kv_local):
        dq, own, rim = attend(qds[c], halo, kv, c, kv_local, low.reshape(1, group), first_tile)
        returned = passed_along(rim, "seq", -1).astype(jnp.float32)
        dkv = jnp.concatenate(
            [own[: group - WINDOW], own[group - WINDOW :] + returned], axis=0
        ).astype(jnp.bfloat16)
        grads.append(to_tokens(jnp.concatenate([dq, dkv], axis=1), ways))

    def gathered(first, last):
        cut = jnp.stack([g[:, :, first:last] for g in grads], axis=2)
        return jnp.transpose(cut, (1, 0, 2, 3)).reshape(tokens, -1)

    q_end = per_group * HD
    return (
        gathered(0, q_end),
        gathered(q_end, q_end + HD),
        gathered(q_end + HD, q_end + 2 * HD),
    )


def solution(mesh):
    rows = P(("seq", "head"), None)
    return jax.shard_map(
        local,
        mesh=mesh,
        in_specs=(rows, rows, rows, rows, P()),
        out_specs=(rows, rows, rows),
        check_vma=False,
    )
```

time: 519 us -> 272 us (0.52)
  matrix products: 188 us -> 0 us
  Pallas kernels: 0 us -> 47.5 us
  other arithmetic: 45.4 us -> 7.23 us
  waiting for transfers between devices: 172 us -> 145 us
  local copies, waits for them, and re-layouts: 52 us -> 28.2 us
  starting transfers between devices: 54.1 us -> 40.4 us
    dot_general x12 -> x0, matrix products: 156 us -> none  [the longest x3 58.3 us: tile_grads(): jnp.einsum('agqk,qagd->kad', grad_scores, q_four, preferred_element_type=...]
    pallas_call x0 -> x2, Pallas kernels: none -> 47.5 us  [attend(): pl.pallas_call(functools.partial(attend_kernel, per_group), grid=(1,), ou...]
    sub x3 -> x0, matrix products: 31.4 us -> none  [tile_grads(): exponent = jnp.exp(scores - row_max)]
    all_to_all x7 -> x5, waiting for transfers between devices: 125 us -> 96.1 us  [the longest x3 63 us: to_heads(): came = lax.all_to_all(sent, 'head', split_axis=0, concat_axis=0, tiled=True)]
    concatenate x4 -> x5, other arithmetic: 28 us -> 6.4 us  [the longest x3 3.85 us: to_heads(): sent = jnp.concatenate([jnp.transpose(p, (1, 0, 2)) for p in parts], axis=2)]
    dynamic_slice x21 -> x0, local copies, waits for them, and re-layouts: 15.6 us -> none  [the longest x3 5.52 us: advance(): value_rows = lax.dynamic_slice_in_dim(value_src, key_first, span, 0)]
    all_to_all x7 -> x5, starting transfers between devices: 48.7 us -> 33.4 us  [the longest x3 20.6 us: to_heads(): came = lax.all_to_all(sent, 'head', split_axis=0, concat_axis=0, tiled=True)]
    all_to_all x7 -> x0, local copies, waits for them, and re-layouts: 10.3 us -> none  [the longest x1 2.71 us: local(): lax.all_to_all(grad_out, 'head', split_axis=1, concat_axis=0, tiled=True)]
  transfers between devices with their start and end apart: 9 -> 8, of which waited for: 8 -> 6; matrix products, arithmetic and copies ran while one was open for 10% -> 4% of each run, Pallas kernels for 0% -> 18%
where the time goes in v1:
time: 272 us; the launch traced here: 269 us
  waiting for transfers between devices  145 us (53%)
  Pallas kernels  47.5 us (17%)
  starting transfers between devices  40.4 us (15%)
  local copies, waits for them, and re-layouts  28.2 us (10%)
  other arithmetic  7.23 us (3%)
    all_to_all x3, waiting for transfers between devices, to_heads(): came = lax.all_to_all(sent, 'head', split_axis=0, concat_axis=0, tiled=True)  63 us
    ppermute x3, waiting for transfers between devices, passed_along(): return lax.ppermute(shard, axis, pairs)  49.1 us
    pallas_call x2, Pallas kernels, attend(): pl.pallas_call(functools.partial(attend_kernel, per_group), grid=(1,), ou...  47.5 us
    all_to_all x2, waiting for transfers between devices, to_tokens(): return lax.all_to_all(sent, 'head', split_axis=0, concat_axis=0, tiled=True)  33.1 us
    all_to_all x3, starting transfers between devices, to_heads(): came = lax.all_to_all(sent, 'head', split_axis=0, concat_axis=0, tiled=True)  20.6 us
    all_to_all x2, starting transfers between devices, to_tokens(): return lax.all_to_all(sent, 'head', split_axis=0, concat_axis=0, tiled=True)  12.8 us
    ppermute x3, starting transfers between devices, passed_along(): return lax.ppermute(shard, axis, pairs)  6.95 us
    slice x2, local copies, waits for them, and re-layouts, local(): qds = [to_heads([q_cut[:, :, c], o_cut[:, :, c]]) for c in range(kv_local)]  6.17 us
  transfers between devices with their start and end apart: 8, of which 6 were waited for; matrix products, arithmetic and copies ran while one was open for 4% of the time, Pallas kernels for 18%

profile of v1, /device:TPU:13, one launch (start us, length us, event | category | flops | bytes accessed | tf_op | source)
XLA Modules:
  0.0 269.3 jit_solution(5281503341231686968)
XLA Ops:
  0.6 2.9 %reshape.95 = bf16[192,8,2,256]{3,2,1,0:T(2,128)(2,1)S(1)} reshape(bf16[192,4096]{1,0:T(8,128)(2,1)} %param.5) | data formatting | bytes 3145728 | tf_op jit(solution)/shard_map/reshape | solution.py:198
  3.5 2.9 %reshape.96 = bf16[192,8,2,256]{3,2,1,0:T(2,128)(2,1)S(1)} reshape(bf16[192,4096]{1,0:T(8,128)(2,1)} %param.8) | data formatting | bytes 3145728 | tf_op jit(solution)/shard_map/reshape | solution.py:199
  6.4 3.1 %fusion.1 = (bf16[192,8,1,256]{3,2,1,0:T(2,128)(2,1)S(1)}, bf16[192,8,1,256]{3,2,1,0:T(2,128)(2,1)}) fusion(bf16[192,8,2,256]{3,2,1,0:T(2,128)(2,1)S(1)} %reshape.96), kind=kLoop, calls=%fused_computation.33 | loop fusion | bytes 3145728 | tf_op jit(solution)/shard_map/slice | solution.py:200
  9.5 3.1 %fusion = (bf16[192,8,1,256]{3,2,1,0:T(2,128)(2,1)S(1)}, bf16[192,8,1,256]{3,2,1,0:T(2,128)(2,1)}) fusion(bf16[192,8,2,256]{3,2,1,0:T(2,128)(2,1)S(1)} %reshape.95), kind=kLoop, calls=%fused_computation.32 | loop fusion | bytes 3145728 | tf_op jit(solution)/shard_map/slice | solution.py:200
  13.4 1.3 pad_maximum_fusion
  14.7 5.8 %all-to-all-start = ((bf16[8,192,512]{2,1,0:T(8,128)(2,1)}), bf16[8,192,512]{2,1,0:T(8,128)(2,1)S(1)}, u32[]{:S(2)}, u32[]{:S(2)}) async-start(bf16[8,192,512]{2,1,0:T(8,128)(2,1)} %pad_maximum_fusion), calls=%async_computation | async-start | bytes 3145728 | tf_op jit(solution)/shard_map/all_to_all | solution.py:179
  20.7 1.3 pad_maximum_fusion.1
  22.0 32.8 %all-to-all-done = bf16[8,192,512]{2,1,0:T(8,128)(2,1)S(1)} async-done(((bf16[8,192,512]{2,1,0:T(8,128)(2,1)}), bf16[8,192,512]{2,1,0:T(8,128)(2,1)S(1)}, u32[]{:S(2)}, u32[]{:S(2)}) %all-to-all-start) | async-done | bytes 1572896 | tf_op jit(solution)/shard_map/all_to_all | solution.py:179
  54.8 7.0 %all-to-all-start.1 = ((bf16[8,192,512]{2,1,0:T(8,128)(2,1)}), bf16[8,192,512]{2,1,0:T(8,128)(2,1)S(1)}, u32[]{:S(2)}, u32[]{:S(2)}) async-start(bf16[8,192,512]{2,1,0:T(8,128)(2,1)} %pad_maximum_fusion.1), calls=%async_computation.1 | async-start | bytes 3145728 | tf_op jit(solution)/shard_map/all_to_all | solution.py:179
  61.8 2.8 %copy_bitcast_fusion = (bf16[8,192,256]{2,1,0:T(8,128)(2,1)S(1)}, bf16[8,192,256]{2,1,0:T(8,128)(2,1)S(1)}) fusion(bf16[192,8,1,256]{3,2,1,0:T(2,128)(2,1)} %get-tuple-element.22, bf16[192,8,1,256]{3,2,1,0:T(2,128)(2,1)} %get-tuple-element.20), kind=kLoop, calls=%fused_computation.14 | loop fusion | bytes 3145728 | tf_op jit(solution)/shard_map/transpose | solution.py:178
  64.6 1.3 pad_maximum_fusion.2
  65.9 30.2 %all-to-all-done.1 = bf16[8,192,512]{2,1,0:T(8,128)(2,1)S(1)} async-done(((bf16[8,192,512]{2,1,0:T(8,128)(2,1)}), bf16[8,192,512]{2,1,0:T(8,128)(2,1)S(1)}, u32[]{:S(2)}, u32[]{:S(2)}) %all-to-all-start.1) | async-done | bytes 1572896 | tf_op jit(solution)/shard_map/all_to_all | solution.py:179
  96.1 7.8 %all-to-all-start.3 = ((bf16[8,192,512]{2,1,0:T(8,128)(2,1)}), bf16[8,192,512]{2,1,0:T(8,128)(2,1)}, u32[]{:S(2)}, u32[]{:S(2)}) async-start(bf16[8,192,512]{2,1,0:T(8,128)(2,1)} %pad_maximum_fusion.2), calls=%async_computation.3 | async-start | bytes 3145728 | tf_op jit(solution)/shard_map/all_to_all | solution.py:179
  104.9 3.1 %collective-permute-start = (bf16[1024,512]{1,0:T(8,128)(2,1)}, bf16[1024,512]{1,0:T(8,128)(2,1)}, u32[]{:S(2)}, u32[]{:S(2)}) collective-permute-start(bf16[1024,512]{1,0:T(8,128)(2,1)} %slice.68), channel_id=1, source_target_pairs={{0,8},{8,16},{16,24},{1,9},{9,17},{17,25},{2,10},{10,18},{18,26},{... | collective-permute-start | bytes 3145736 | tf_op jit(solution)/shard_map/ppermute | solution.py:23
  108.6 23.9 %collective-permute-done.halo_k.halo_v = bf16[1024,512]{1,0:T(8,128)(2,1)} collective-permute-done((bf16[1024,512]{1,0:T(8,128)(2,1)}, bf16[1024,512]{1,0:T(8,128)(2,1)}, u32[]{:S(2)}, u32[]{:S(2)}) %collective-permute-start) | collective-permute-done | bytes 1048608 | tf_op jit(solution)/shard_map/ppermute | solution.py:23
  132.4 23.5 %attend.2 = (bf16[1536,256]{1,0:T(8,128)(2,1)S(1)}, f32[1536,256]{1,0:T(8,128)S(1)}, bf16[1024,256]{1,0:T(8,128)(2,1)S(1)}) custom-call(s32[6]{0:T(128)S(1)} %and_select_fusion.first_tile, s32[1,1536]{1,0:T(1,128)S(1)} %maximum_subtract_fusion.1.low_ref, bf16[1536,512]{1,0:T(8,128)(2,1)S(1)} %bitcast.55, ...), custom_call_target="tpu_custom_call" | custom-call | flops 5033164800 | bytes 4718592 | tf_op jit(solution)/shard_map/attend/pallas_call | solution.py:137
  155.9 1.9 collective-permute-start.1
  157.9 12.1 %collective-permute-done.1 = bf16[1024,256]{1,0:T(8,128)(2,1)S(1)} collective-permute-done((bf16[1024,256]{1,0:T(8,128)(2,1)S(1)}, bf16[1024,256]{1,0:T(8,128)(2,1)S(1)}, u32[]{:S(2)}, u32[]{:S(2)}) %collective-permute-start.1) | collective-permute-done | bytes 524320 | tf_op jit(solution)/shard_map/ppermute | solution.py:23
  170.1 1.3 maximum_maximum_fusion
  171.4 6.9 %all-to-all-start.2 = ((bf16[8,192,512]{2,1,0:T(8,128)(2,1)}), bf16[8,192,512]{2,1,0:T(8,128)(2,1)}, u32[]{:S(2)}, u32[]{:S(2)}) async-start(bf16[8,192,512]{2,1,0:T(8,128)(2,1)} %bitcast.9), calls=%async_computation.2 | async-start | bytes 3145728 | tf_op jit(solution)/shard_map/all_to_all | solution.py:185
  178.3 24.0 %attend.3 = (bf16[1536,256]{1,0:T(8,128)(2,1)S(1)}, f32[1536,256]{1,0:T(8,128)S(1)}, bf16[1024,256]{1,0:T(8,128)(2,1)S(1)}) custom-call(s32[6]{0:T(128)S(1)} %and_select_fusion.first_tile, s32[1,1536]{1,0:T(1,128)S(1)} %maximum_subtract_fusion.1.low_ref, bf16[1536,512]{1,0:T(8,128)(2,1)} %bitcast.15.qd_ref, ...), custom_call_target="tpu_custom_call" | custom-call | flops 5033164800 | bytes 4718592 | tf_op jit(solution)/shard_map/attend/pallas_call | solution.py:137
  202.3 1.9 collective-permute-start.2
  204.3 13.1 %collective-permute-done.2 = bf16[1024,256]{1,0:T(8,128)(2,1)S(1)} collective-permute-done((bf16[1024,256]{1,0:T(8,128)(2,1)S(1)}, bf16[1024,256]{1,0:T(8,128)(2,1)S(1)}, u32[]{:S(2)}, u32[]{:S(2)}) %collective-permute-start.2) | collective-permute-done | bytes 524320 | tf_op jit(solution)/shard_map/ppermute | solution.py:23
  217.5 1.3 maximum_maximum_fusion.1
  218.8 5.9 %all-to-all-start.4 = ((bf16[8,192,512]{2,1,0:T(8,128)(2,1)}), bf16[8,192,512]{2,1,0:T(8,128)(2,1)S(1)}, u32[]{:S(2)}, u32[]{:S(2)}) async-start(bf16[8,192,512]{2,1,0:T(8,128)(2,1)} %bitcast.56), calls=%async_computation.4 | async-start | bytes 3145728 | tf_op jit(solution)/shard_map/all_to_all | solution.py:185
  224.7 1.2 slice_bitcast_fusion.3
  225.9 33.1 %all-to-all-done.4 = bf16[8,192,512]{2,1,0:T(8,128)(2,1)S(1)} async-done(((bf16[8,192,512]{2,1,0:T(8,128)(2,1)}), bf16[8,192,512]{2,1,0:T(8,128)(2,1)S(1)}, u32[]{:S(2)}, u32[]{:S(2)}) %all-to-all-start.4) | async-done | bytes 1572896 | tf_op jit(solution)/shard_map/all_to_all | solution.py:185
  260.1 1.5 reshape.106
  261.5 1.2 slice_bitcast_fusion.1
  262.9 1.6 copy.35
  264.6 2.4 reshape.104
  267.9 1.5 reshape.105
  (31 shorter events, 5.0 us)
Async XLA Ops:
  14.7 5.8 %copy-start = (bf16[192,2048]{1,0:T(8,128)(2,1)S(1)}, bf16[192,2048]{1,0:T(8,128)(2,1)}, u32[]{:S(2)}) copy-start(bf16[192,2048]{1,0:T(8,128)(2,1)} %param.7) | copy-start | bytes 2359300
  14.7 5.8 %copy-start.1 = (bf16[192,2048]{1,0:T(8,128)(2,1)S(1)}, bf16[192,2048]{1,0:T(8,128)(2,1)}, u32[]{:S(2)}) copy-start(bf16[192,2048]{1,0:T(8,128)(2,1)} %param.6) | copy-start | bytes 2359300
  14.7 40.0 %all-to-all-start = ((bf16[8,192,512]{2,1,0:T(8,128)(2,1)}), bf16[8,192,512]{2,1,0:T(8,128)(2,1)S(1)}, u32[]{:S(2)}, u32[]{:S(2)}) async-start(bf16[8,192,512]{2,1,0:T(8,128)(2,1)} %pad_maximum_fusion), calls=%async_computation | async-start | bytes 3145728 | tf_op jit(solution)/shard_map/all_to_all | solution.py:179
  54.8 41.3 %all-to-all-start.1 = ((bf16[8,192,512]{2,1,0:T(8,128)(2,1)}), bf16[8,192,512]{2,1,0:T(8,128)(2,1)S(1)}, u32[]{:S(2)}, u32[]{:S(2)}) async-start(bf16[8,192,512]{2,1,0:T(8,128)(2,1)} %pad_maximum_fusion.1), calls=%async_computation.1 | async-start | bytes 3145728 | tf_op jit(solution)/shard_map/all_to_all | solution.py:179
  96.1 75.3 %all-to-all-start.3 = ((bf16[8,192,512]{2,1,0:T(8,128)(2,1)}), bf16[8,192,512]{2,1,0:T(8,128)(2,1)}, u32[]{:S(2)}, u32[]{:S(2)}) async-start(bf16[8,192,512]{2,1,0:T(8,128)(2,1)} %pad_maximum_fusion.2), calls=%async_computation.3 | async-start | bytes 3145728 | tf_op jit(solution)/shard_map/all_to_all | solution.py:179
  103.9 4.2 %copy-start.2 = (s32[16]{0:T(128)S(1)}, s32[16]{0:T(128)}, u32[]{:S(2)}) copy-start(s32[16]{0:T(128)} %param.9) | copy-start | bytes 196
  104.9 27.5 %collective-permute-start = (bf16[1024,512]{1,0:T(8,128)(2,1)}, bf16[1024,512]{1,0:T(8,128)(2,1)}, u32[]{:S(2)}, u32[]{:S(2)}) collective-permute-start(bf16[1024,512]{1,0:T(8,128)(2,1)} %slice.68), channel_id=1, source_target_pairs={{0,8},{8,16},{16,24},{1,9},{9,17},{17,25},{2,10},{10,18},{18,26},{... | collective-permute-start | bytes 3145736 | tf_op jit(solution)/shard_map/ppermute | solution.py:23
  155.9 14.1 %collective-permute-start.1 = (bf16[1024,256]{1,0:T(8,128)(2,1)S(1)}, bf16[1024,256]{1,0:T(8,128)(2,1)S(1)}, u32[]{:S(2)}, u32[]{:S(2)}) collective-permute-start(bf16[1024,256]{1,0:T(8,128)(2,1)S(1)} %get-tuple-element.11), channel_id=1, source_target_pairs={{8,0},{16,8},{24,16},{9,1},{17,9},{25,17},{10,2},{18,10},{26,18},{... | collective-permute-start | bytes 1572872 | tf_op jit(solution)/shard_map/ppermute | solution.py:23
  171.4 47.3 %all-to-all-start.2 = ((bf16[8,192,512]{2,1,0:T(8,128)(2,1)}), bf16[8,192,512]{2,1,0:T(8,128)(2,1)}, u32[]{:S(2)}, u32[]{:S(2)}) async-start(bf16[8,192,512]{2,1,0:T(8,128)(2,1)} %bitcast.9), calls=%async_computation.2 | async-start | bytes 3145728 | tf_op jit(solution)/shard_map/all_to_all | solution.py:185
  202.3 15.0 %collective-permute-start.2 = (bf16[1024,256]{1,0:T(8,128)(2,1)S(1)}, bf16[1024,256]{1,0:T(8,128)(2,1)S(1)}, u32[]{:S(2)}, u32[]{:S(2)}) collective-permute-start(bf16[1024,256]{1,0:T(8,128)(2,1)S(1)} %get-tuple-element.14), channel_id=1, source_target_pairs={{8,0},{16,8},{24,16},{9,1},{17,9},{25,17},{10,2},{18,10},{26,18},{... | collective-permute-start | bytes 1572872 | tf_op jit(solution)/shard_map/ppermute | solution.py:23
  218.8 40.2 %all-to-all-start.4 = ((bf16[8,192,512]{2,1,0:T(8,128)(2,1)}), bf16[8,192,512]{2,1,0:T(8,128)(2,1)S(1)}, u32[]{:S(2)}, u32[]{:S(2)}) async-start(bf16[8,192,512]{2,1,0:T(8,128)(2,1)} %bitcast.56), calls=%async_computation.4 | async-start | bytes 3145728 | tf_op jit(solution)/shard_map/all_to_all | solution.py:185
